TPU v7x, 32 devices: a whole 2x2x4 slice. The times are simulated.
32 devices in a mesh: groups: 2 (over x), tile: 16 (over z, y, core).
Axes of the slice: x: 2, y: 2, z: 4, core: 2. Of those that a mesh axis runs over, the one named last changes fastest.
Arguments:
- tile_values: bfloat16 [320, 512, 512], P(('groups', 'tile')), parts along dimension 0, may hold values from 0.05 to 5
- tile_rows: int32 [320], P(('groups', 'tile')), parts along dimension 0, may hold values from 0 to 15, as said below
- tile_cols: int32 [320], P(('groups', 'tile')), parts along dimension 0, may hold values from 0 to 15
- tile_live: int32 [320], P(('groups', 'tile')), parts along dimension 0, may hold values from 0 to 1, as said below
- bias: float32 [32, 512], P(('groups', 'tile')), parts along dimension 0, may hold values from 0.5 to 2
Outputs:
- balanced: float32 [32, 512], P(('groups', 'tile')), parts along dimension 0
- coverage: float32 [32, 512], P(('groups', 'tile')), parts along dimension 0
There are 2 independent parts, one for each index of `groups`. A program takes and returns all parts, laid end to end along the dimension named above; each array names one. Nothing has to cross between parts.
Inputs may be any that keep to these rules, and one draw needn't show every extreme that they name: `tile_live`: within each device's 10 slots the live ones come first. Device d holds the band tiles of its own 1 bin blocks (row block owned, column block minus row block 0 to 7, within the map), then 0 to 2 trans tiles; every bin block has its diagonal tile; some device has all 10 slots live. On live slots tile_rows <= tile_cols; trans tiles lie anywhere.
All inputs are finite; a program needn't handle non-finite values.
Results may differ from a plain program's by a relative error of at most 0.00035.
Values sent between devices are 32-bit elements; how exact they have to be, the bound alone decides.
A program may use at most 64 MiB of HBM per device.

v0:
```python
import jax
import jax.numpy as jnp
from jax import lax
from jax.sharding import PartitionSpec as P

ITERS = 2


def split_pair(vector):
    upper_part = vector.astype(jnp.bfloat16)
    lower_part = (vector - upper_part.astype(jnp.float32)).astype(jnp.bfloat16)
    return jnp.stack([upper_part, lower_part])


def local_margin(tile_values, tile_rows, tile_cols, live_total, scales_all):

    def visit_tile(index, totals):
        matrix = lax.dynamic_index_in_dim(tile_values, index, 0, keepdims=False)
        row_block = tile_rows[index]
        col_block = tile_cols[index]
        weight = jnp.where(row_block == col_block, 0.5, 1.0).astype(jnp.float32)
        row_pair = split_pair(lax.dynamic_index_in_dim(scales_all, row_block, 0, keepdims=False))
        col_pair = split_pair(lax.dynamic_index_in_dim(scales_all, col_block, 0, keepdims=False))
        to_rows = (
            jnp.sum(
                lax.dot_general(
                    col_pair, matrix, (((1,), (1,)), ((), ())), preferred_element_type=jnp.float32
                ),
                axis=0,
            )
            * weight
        )
        to_cols = (
            jnp.sum(jnp.dot(row_pair, matrix, preferred_element_type=jnp.float32), axis=0) * weight
        )
        totals = totals.at[row_block].add(to_rows)
        totals = totals.at[col_block].add(to_cols)
        return totals

    start = jnp.zeros(scales_all.shape, jnp.float32)
    return lax.fori_loop(0, live_total, visit_tile, start)


def shards(tile_values, tile_rows, tile_cols, tile_live, bias):
    owned_blocks = bias.shape[0]
    tile_width = bias.shape[1]
    device_total = lax.axis_size("tile")
    block_total = owned_blocks * device_total
    live_total = jnp.sum(tile_live)
    scales = bias
    coverage = bias
    for sweep in range(ITERS):
        scales_all = lax.all_gather(scales, "tile", axis=0, tiled=True)
        partial_sums = local_margin(tile_values, tile_rows, tile_cols, live_total, scales_all)
        owned = lax.psum_scatter(partial_sums, "tile", scatter_dimension=0, tiled=True)
        margin = scales * owned
        grand = lax.psum(jnp.sum(margin), "tile")
        average = grand / (block_total * tile_width)
        coverage = margin / average
        scales = scales / coverage
    return (scales, coverage)


def solution(mesh):
    placed = (
        P(("groups", "tile"), None, None),
        P(("groups", "tile")),
        P(("groups", "tile")),
        P(("groups", "tile")),
        P(("groups", "tile"), None),
    )
    return jax.shard_map(
        shards,
        mesh=mesh,
        in_specs=placed,
        out_specs=(P(("groups", "tile"), None), P(("groups", "tile"), None)),
        check_vma=False,
    )
```

profile of v0, /device:TPU:0, one launch (start us, length us, event | category | flops | bytes accessed | tf_op | source)
XLA Modules:
  0.0 500.8 jit_solution(9608238890214082236)
XLA Ops:
  0.6 1.3 dynamic-slice.40
  3.3 23.4 %all-gather = f32[16,1,512]{2,1,0:T(1,128)S(1)} all-gather(f32[1,1,512]{2,1,0:T(1,128)} %bitcast.69), channel_id=1, replica_groups=mesh['groups'=2,'tile'=16] {'tile'}, dimensions={0}, use_global_device_ids=true | all-gather | bytes 34816 | tf_op jit(solution)/shard_map/all_gather | solution.py:53
  26.7 136.9 %while.24 = (s32[]{:T(128)}, f32[16,512]{1,0:T(8,128)S(1)}, s32[]{:T(128)}, s32[10]{0:T(128)}, s32[10]{0:T(128)}, /*index=5*/f32[16,512]{1,0:T(8,128)S(1)}, bf16...) while((s32[]{:T(128)}, f32[16,512]{1,0:T(8,128)S(1)}, ...), condition=%wide.region_6.7_spmd, body=%wide.region_1.6_spmd.sunk | while | flops 2113567 | bytes 1096045 | solution.py:41
  27.3 1.3 dynamic_slice.93
  34.9 1.4 and_reduce_fusion.6
  41.0 1.3 dynamic_slice.93
  48.5 1.4 and_reduce_fusion.6
  54.6 1.3 dynamic_slice.93
  62.1 1.4 and_reduce_fusion.6
  68.2 1.3 dynamic_slice.93
  75.8 1.4 and_reduce_fusion.6
  81.8 1.3 dynamic_slice.93
  89.4 1.4 and_reduce_fusion.6
  95.5 1.3 dynamic_slice.93
  103.0 1.4 and_reduce_fusion.6
  109.1 1.3 dynamic_slice.93
  116.6 1.4 and_reduce_fusion.6
  122.7 1.3 dynamic_slice.93
  130.3 1.4 and_reduce_fusion.6
  136.3 1.3 dynamic_slice.93
  143.9 1.4 and_reduce_fusion.6
  150.0 1.3 dynamic_slice.93
  157.5 1.4 and_reduce_fusion.6
  163.6 57.6 %all-reduce = f32[16,512]{1,0:T(8,128)S(1)} all-reduce(f32[16,512]{1,0:T(8,128)S(1)} %get-tuple-element.126), channel_id=2, replica_groups=mesh['groups'=2,'tile'=16] {'tile'}, use_global_device_ids=true, to_apply=%region_7.8.clone | all-reduce | flops 8192 | bytes 65536
  222.5 30.1 %psum.14 = f32[]{:T(128)} all-reduce(f32[]{:T(128)} %fusion.32), channel_id=1, replica_groups=mesh['groups'=2,'tile'=16] {'tile'}, use_global_device_ids=true, to_apply=%region_9.10 | all-reduce | flops 1 | bytes 8 | tf_op jit(solution)/shard_map/psum | solution.py:57
  254.0 17.2 %all-gather.1 = f32[16,1,512]{2,1,0:T(1,128)S(1)} all-gather(f32[1,1,512]{2,1,0:T(1,128)S(1)} %bitcast.70), channel_id=1, replica_groups=mesh['groups'=2,'tile'=16] {'tile'}, dimensions={0}, use_global_device_ids=true | all-gather | bytes 34816 | tf_op jit(solution)/shard_map/all_gather | solution.py:53
  271.2 138.6 %while.25 = (s32[]{:T(128)}, f32[16,512]{1,0:T(8,128)S(1)}, s32[]{:T(128)}, s32[10]{0:T(128)}, s32[10]{0:T(128)}, /*index=5*/f32[16,512]{1,0:T(8,128)S(1)}, bf16...) while((s32[]{:T(128)}, f32[16,512]{1,0:T(8,128)S(1)}, ...), condition=%wide.region_15.16_spmd, body=%wide.region_10.15_spmd.sunk | while | flops 2113567 | bytes 1096045 | solution.py:41
  271.9 1.3 dynamic_slice.99
  279.5 1.4 and_reduce_fusion.7
  285.6 1.3 dynamic_slice.99
  293.3 1.4 and_reduce_fusion.7
  299.4 1.3 dynamic_slice.99
  307.1 1.4 and_reduce_fusion.7
  313.2 1.3 dynamic_slice.99
  320.9 1.4 and_reduce_fusion.7
  327.0 1.3 dynamic_slice.99
  334.7 1.4 and_reduce_fusion.7
  340.8 1.3 dynamic_slice.99
  348.5 1.4 and_reduce_fusion.7
  354.6 1.3 dynamic_slice.99
  362.3 1.4 and_reduce_fusion.7
  368.4 1.3 dynamic_slice.99
  376.1 1.4 and_reduce_fusion.7
  389.9 1.4 and_reduce_fusion.7
  396.0 1.3 dynamic_slice.99
  403.7 1.4 and_reduce_fusion.7
  409.8 57.6 %all-reduce.1 = f32[16,512]{1,0:T(8,128)S(1)} all-reduce(f32[16,512]{1,0:T(8,128)S(1)} %get-tuple-element.127), channel_id=3, replica_groups=mesh['groups'=2,'tile'=16] {'tile'}, use_global_device_ids=true, to_apply=%region_16.17.clone | all-reduce | flops 8192 | bytes 65536
  468.7 30.1 %psum.15 = f32[]{:T(128)} all-reduce(f32[]{:T(128)} %get-tuple-element.160), channel_id=1, replica_groups=mesh['groups'=2,'tile'=16] {'tile'}, use_global_device_ids=true, to_apply=%region_18.19 | all-reduce | flops 1 | bytes 8 | tf_op jit(solution)/shard_map/psum | solution.py:57
  (212 shorter events, 111.4 us)
Async XLA Ops:
  0.6 220.6 %copy-start = (f32[1,512]{1,0:T(1,128)S(1)}, f32[1,512]{1,0:T(1,128)}, u32[]{:S(2)}) copy-start(f32[1,512]{1,0:T(1,128)} %param.21) | copy-start | bytes 6148
where the time goes:
time: 500 us; the launch traced here: 501 us
  blocking collectives  216 us (43%)
  loops' own time  117 us (23%)
  other arithmetic  59.8 us (12%)
  local copies, waits for them, and re-layouts  55.3 us (11%)
  matrix products  50.7 us (10%)
    another operation x2, loops' own time, local_margin(): return lax.fori_loop(0, live_total, visit_tile, start)  117 us
    unnamed x2, blocking collectives  115 us
    psum x2, blocking collectives, shards(): grand = lax.psum(jnp.sum(margin), 'tile')  60.2 us
    another operation x60, other arithmetic  53.4 us
    all_gather x2, blocking collectives, shards(): scales_all = lax.all_gather(scales, 'tile', axis=0, tiled=True)  40.6 us
    dynamic_slice x20, local copies, waits for them, and re-layouts, visit_tile(): row_block = tile_rows[index]  26.1 us
    dot_general x20, matrix products, visit_tile(): lax.dot_general(col_pair, matrix, (((1,), (1,)), ((), ())), preferred_ele...  26 us
    dynamic_slice x20, local copies, waits for them, and re-layouts, visit_tile(): col_block = tile_cols[index]  25.2 us

commit v1 on v0

v1 whole, which is shorter than its diff:
```python
import functools

import jax
import jax.numpy as jnp
from jax import lax
from jax.experimental import pallas as pl
from jax.experimental.pallas import tpu as pltpu
from jax.sharding import PartitionSpec as P

ITERS = 2
BAND = 8
TRANS = 2
LANES = 128
MESH = pl.DeviceIdType.MESH


def each_peer(me, n, body):
    if n <= 16:
        for step in range(1, n):
            body(lax.rem(me + step, n))
    else:

        @pl.loop(1, n)
        def _(step):
            body(lax.rem(me + step, n))


def kernel(
    n, values, rows_in, cols_in, live_in, bias_in, balanced, coverage,
    tiles, rows, cols, live, bias, scales0, scales1, send0, send1, recv0, recv1,
    tile_sem, small_sem, out_sem, in_sem,
):
    group = lax.axis_index("groups")
    me = lax.axis_index("tile")
    slots, width = values.shape[0], values.shape[1]
    parts = width // LANES
    messages = parts + 1

    smalls = [
        pltpu.make_async_copy(source, target, small_sem.at[index])
        for index, (source, target) in enumerate(
            ((bias_in, bias), (rows_in, rows), (cols_in, cols), (live_in, live))
        )
    ]
    loads = [
        pltpu.make_async_copy(values.at[slot], tiles.at[slot], tile_sem.at[slot])
        for slot in range(slots)
    ]
    for copy in smalls + loads:
        copy.start()

    barrier = pltpu.get_barrier_semaphore()
    each_peer(
        me,
        n,
        lambda peer: pl.semaphore_signal(
            barrier, inc=1, device_id=(group, peer), device_id_type=MESH
        ),
    )

    smalls[0].wait()
    for part in range(parts):
        scales0[me, part : part + 1, :] = bias[:, part * LANES : (part + 1) * LANES]
    pl.semaphore_wait(barrier, n - 1)

    def gather_start(scales, phase):
        each_peer(
            me,
            n,
            lambda peer: pltpu.make_async_remote_copy(
                src_ref=scales.at[me],
                dst_ref=scales.at[me],
                send_sem=out_sem.at[phase],
                recv_sem=in_sem.at[phase],
                device_id=(group, peer),
                device_id_type=MESH,
            ).start(),
        )

    def reduce_start(send, recv, phase):
        each_peer(
            me,
            n,
            lambda peer: pltpu.make_async_remote_copy(
                src_ref=send.at[peer],
                dst_ref=recv.at[me],
                send_sem=out_sem.at[phase],
                recv_sem=in_sem.at[phase],
                device_id=(group, peer),
                device_id_type=MESH,
            ).start(),
        )

    def arrived(buffer, sem):
        every = buffer.at[pl.ds(0, n - 1)]
        pltpu.make_async_copy(every, every, sem).wait()

    def as_row(buffer, index):
        return jnp.concatenate(
            [buffer[index, part : part + 1, :] for part in range(parts)], axis=1
        )

    def halves(vector):
        upper = vector.astype(jnp.bfloat16).astype(jnp.float32)
        return upper, vector - upper

    place = lax.broadcasted_iota(jnp.int32, (2 * n, width), 0)
    is_upper = place < n
    owner = jnp.where(is_upper, place, place - n)
    line = lax.broadcasted_iota(jnp.int32, (16, width), 0)

    def for_owner(vector, weight, target):
        upper, lower = halves(vector * weight)
        pair = jnp.where(is_upper, upper, lower)
        return jnp.where(owner == target, pair, 0.0).astype(jnp.bfloat16)

    def as_pair(vector, weight):
        upper, lower = halves(vector * weight)
        pair = jnp.where(line == 0, upper, jnp.where(line == 1, lower, 0.0))
        return pair.astype(jnp.bfloat16)

    def times(left, slot):
        return jnp.dot(left, tiles[slot], preferred_element_type=jnp.float32)

    def times_transposed(left, slot):
        return lax.dot_general(
            left, tiles[slot], (((1,), (1,)), ((), ())), preferred_element_type=jnp.float32
        )

    held = jnp.minimum(BAND, n - me)
    grands = []
    mine = None
    for sweep, (scales, send, recv) in enumerate(
        ((scales0, send0, recv0), (scales1, send1, recv1))
    ):
        gather_start(scales, 2 * sweep)
        if sweep == 0:
            for copy in smalls[1:]:
                copy.wait()
            mine = scales[me, 0:parts, :]
        band_cols = [cols[slot] for slot in range(BAND)]
        band_weights = [
            jnp.where(band_cols[slot] == me, 0.5, 1.0)
            * jnp.where(slot < held, 1.0, 0.0)
            for slot in range(BAND)
        ]
        own_row = as_row(scales, me)
        to_cols = jnp.zeros((2 * n, width), jnp.float32)
        for slot in range(BAND):
            if sweep == 0:
                loads[slot].wait()
            to_cols += times(for_owner(own_row, band_weights[slot], band_cols[slot]), slot)
        if sweep == 0:
            for copy in loads[BAND:]:
                copy.wait()

        arrived(scales, in_sem.at[2 * sweep])
        to_rows = jnp.zeros((n, width), jnp.float32)
        for extra in range(TRANS):
            slot = held + extra
            row, col = rows[slot], cols[slot]
            weight = jnp.where(row == col, 0.5, 1.0) * live[slot].astype(jnp.float32)
            to_cols += times(for_owner(as_row(scales, row), weight, col), slot)
            found = times_transposed(as_pair(as_row(scales, col), weight), slot)
            found = found[0:1] + found[1:2]
            to_rows += jnp.where(owner[:n] == row, found, 0.0)
        once = to_cols[:n] + to_cols[n:]
        both = once + to_rows
        flat_scales = scales.reshape(n * 8, LANES)
        flat_send = send.reshape(n * 8, LANES)
        form = jnp.zeros((n, LANES), jnp.float32)
        for part in range(parts):
            lanes = slice(part * LANES, (part + 1) * LANES)
            flat_send[pl.ds(part, n, stride=8), :] = both[:, lanes]
            form += once[:, lanes] * flat_scales[pl.ds(part, n, stride=8), :]
        form = jnp.sum(form, axis=0, keepdims=True)
        flat_send[pl.ds(parts, n, stride=8), :] = jnp.broadcast_to(form, (n, LANES))
        reduce_start(send, recv, 2 * sweep + 1)

        owned = jnp.zeros((16, width), jnp.float32)
        for slot in range(BAND):
            pair = as_pair(as_row(scales, band_cols[slot]), band_weights[slot])
            owned += times_transposed(pair, slot)
        owned = owned[0:1] + owned[1:2]
        owned += jnp.sum(jnp.where(owner[:n] == me, both, 0.0), axis=0, keepdims=True)
        for part in range(parts):
            recv[me, part : part + 1, :] = owned[:, part * LANES : (part + 1) * LANES]
        recv[me, parts:messages, :] = form
        arrived(recv, in_sem.at[2 * sweep + 1])
        total = jnp.sum(recv[:, 0:messages, :], axis=0)
        grands.append(2.0 * jnp.sum(total[parts:messages], keepdims=True))
        total = total[0:parts]
        if sweep + 1 < ITERS:
            mine = 1.0 / total
            scales1[me, 0:parts, :] = mine

    bins = float(n * width)
    over = mine * total * (bins / grands[1])
    result = mine * (grands[0] / bins) / over
    for part in range(parts):
        lanes = slice(part * LANES, (part + 1) * LANES)
        coverage[:, lanes] = over[part : part + 1]
        balanced[:, lanes] = result[part : part + 1]
    for phase, buffer in enumerate((scales0, send0, scales1, send1)):
        arrived(buffer, out_sem.at[phase])


def solution(mesh):
    n = mesh.shape["tile"]

    def shards(tile_values, tile_rows, tile_cols, tile_live, bias):
        slots, width = tile_values.shape[0], tile_values.shape[1]
        block = pltpu.VMEM((n, 8, LANES), jnp.float32)
        return pl.pallas_call(
            functools.partial(kernel, n),
            out_shape=(jax.ShapeDtypeStruct(bias.shape, jnp.float32),) * 2,
            in_specs=[pl.BlockSpec(memory_space=pltpu.HBM)] * 5,
            out_specs=(pl.BlockSpec(memory_space=pltpu.VMEM),) * 2,
            scratch_shapes=[
                pltpu.VMEM((slots, width, width), jnp.bfloat16),
                pltpu.SMEM((slots,), jnp.int32),
                pltpu.SMEM((slots,), jnp.int32),
                pltpu.SMEM((slots,), jnp.int32),
                pltpu.VMEM(bias.shape, jnp.float32),
                block, block, block, block, block, block,
                pltpu.SemaphoreType.DMA((slots,)),
                pltpu.SemaphoreType.DMA((4,)),
                pltpu.SemaphoreType.DMA((4,)),
                pltpu.SemaphoreType.DMA((4,)),
            ],
            compiler_params=pltpu.CompilerParams(
                collective_id=0, has_side_effects=True, vmem_limit_bytes=48 * 1024 * 1024
            ),
        )(tile_values, tile_rows, tile_cols, tile_live, bias)

    placed = (
        P(("groups", "tile"), None, None),
        P(("groups", "tile")),
        P(("groups", "tile")),
        P(("groups", "tile")),
        P(("groups", "tile"), None),
    )
    return jax.shard_map(
        shards,
        mesh=mesh,
        in_specs=placed,
        out_specs=(P(("groups", "tile"), None), P(("groups", "tile"), None)),
        check_vma=False,
    )
```

time: 500 us -> 31.7 us (0.06)
  blocking collectives: 216 us -> 0 us
  loops' own time: 117 us -> 0 us
  other arithmetic: 59.8 us -> 0 us
  matrix products: 50.7 us -> 0 us
  local copies, waits for them, and re-layouts: 55.3 us -> 6.28 us
  Pallas kernels: 0 us -> 24.6 us
    another operation x2 -> x0, loops' own time: 117 us -> none  [local_margin(): return lax.fori_loop(0, live_total, visit_tile, start)]
    unnamed x2 -> x0, blocking collectives: 115 us -> none
    psum x2 -> x0, blocking collectives: 60.2 us -> none  [shards(): grand = lax.psum(jnp.sum(margin), 'tile')]
    another operation x60 -> x0, other arithmetic: 53.4 us -> none
    dynamic_slice x40 -> x0, local copies, waits for them, and re-layouts: 51.3 us -> none  [the longest x20 26.1 us: visit_tile(): row_block = tile_rows[index]]
    dot_general x40 -> x0, matrix products: 50.7 us -> none  [the longest x20 26 us: visit_tile(): lax.dot_general(col_pair, matrix, (((1,), (1,)), ((), ())), preferred_ele...]
    all_gather x2 -> x0, blocking collectives: 40.6 us -> none  [shards(): scales_all = lax.all_gather(scales, 'tile', axis=0, tiled=True)]
    pallas_call x0 -> x1, Pallas kernels: none -> 24.6 us  [shards(): pl.pallas_call(functools.partial(kernel, n), out_shape=(jax.ShapeDtypeStr...]
where the time goes in v1:
time: 31.7 us; the launch traced here: 31.5 us
  Pallas kernels  24.6 us (78%)
  local copies, waits for them, and re-layouts  6.28 us (20%)
  between operations  0.65 us (2%)
    pallas_call x1, Pallas kernels, shards(): pl.pallas_call(functools.partial(kernel, n), out_shape=(jax.ShapeDtypeStr...  24.6 us
    unnamed x12, local copies, waits for them, and re-layouts  6.28 us

profile of v1, /device:TPU:0, one launch (start us, length us, event | category | flops | bytes accessed | tf_op | source)
XLA Modules:
  0.0 31.5 jit_solution(9765488585787021471)
XLA Ops:
  0.6 0.0 copy-start
  0.6 2.5 %copy-done = bf16[10,512,512]{2,1,0:T(8,128)(2,1)S(1)} copy-done((bf16[10,512,512]{2,1,0:T(8,128)(2,1)S(1)}, bf16[10,512,512]{2,1,0:T(8,128)(2,1)}, u32[]{:S(2)}) %copy-start) | copy-done | bytes 5242904
  3.1 0.0 copy-start.1
  3.1 0.7 %copy-done.1 = f32[1,512]{1,0:T(1,128)S(1)} copy-done((f32[1,512]{1,0:T(1,128)S(1)}, f32[1,512]{1,0:T(1,128)}, u32[]{:S(2)}) %copy-start.1) | copy-done | bytes 2072
  3.8 0.0 copy-start.2
  3.8 0.7 %copy-done.2 = s32[10]{0:T(128)S(1)} copy-done((s32[10]{0:T(128)S(1)}, s32[10]{0:T(128)}, u32[]{:S(2)}) %copy-start.2) | copy-done | bytes 64
  4.5 0.0 copy-start.3
  4.5 0.7 %copy-done.3 = s32[10]{0:T(128)S(1)} copy-done((s32[10]{0:T(128)S(1)}, s32[10]{0:T(128)}, u32[]{:S(2)}) %copy-start.3) | copy-done | bytes 64
  5.1 0.0 copy-start.4
  5.1 0.7 %copy-done.4 = s32[10]{0:T(128)S(1)} copy-done((s32[10]{0:T(128)S(1)}, s32[10]{0:T(128)}, u32[]{:S(2)}) %copy-start.4) | copy-done | bytes 64
  5.8 24.6 %shard_map.68 = (f32[1,512]{1,0:T(1,128)S(1)}, f32[1,512]{1,0:T(1,128)S(1)}) custom-call(bf16[10,512,512]{2,1,0:T(8,128)(2,1)S(1)} %copy-done, s32[10]{0:T(128)S(1)} %copy-done.2, s32[10]{0:T(128)S(1)} %copy-done.3, s32[10]{0:T(128)S(1)} %copy-done.4, f32[1,512]{1,0:T(1,128)S(1)} %copy-done.1), custom_call_target="tpu_custom_call" | custom-call | tf_op jit(solution)/shard_map/pallas_call | solution.py:214
  30.3 0.6 %copy.9 = f32[1,512]{1,0:T(1,128)} copy(f32[1,512]{1,0:T(1,128)S(1)} %get-tuple-element.4) | data formatting | bytes 4096
  30.9 0.6 %copy.10 = f32[1,512]{1,0:T(1,128)} copy(f32[1,512]{1,0:T(1,128)S(1)} %get-tuple-element.5) | data formatting | bytes 4096
Async XLA Ops:
  0.6 2.5 %copy-start = (bf16[10,512,512]{2,1,0:T(8,128)(2,1)S(1)}, bf16[10,512,512]{2,1,0:T(8,128)(2,1)}, u32[]{:S(2)}) copy-start(bf16[10,512,512]{2,1,0:T(8,128)(2,1)} %values.1) | copy-start | bytes 15728644
  3.1 0.7 %copy-start.1 = (f32[1,512]{1,0:T(1,128)S(1)}, f32[1,512]{1,0:T(1,128)}, u32[]{:S(2)}) copy-start(f32[1,512]{1,0:T(1,128)} %bias_in.1) | copy-start | bytes 6148
  3.8 0.7 %copy-start.2 = (s32[10]{0:T(128)S(1)}, s32[10]{0:T(128)}, u32[]{:S(2)}) copy-start(s32[10]{0:T(128)} %rows_in.1) | copy-start | bytes 124
  4.5 0.7 %copy-start.3 = (s32[10]{0:T(128)S(1)}, s32[10]{0:T(128)}, u32[]{:S(2)}) copy-start(s32[10]{0:T(128)} %cols_in.1) | copy-start | bytes 124
  5.1 0.7 %copy-start.4 = (s32[10]{0:T(128)S(1)}, s32[10]{0:T(128)}, u32[]{:S(2)}) copy-start(s32[10]{0:T(128)} %live_in.1) | copy-start | bytes 124

commit v2 on v1

--- a/solution.py
+++ b/solution.py
@@ -15,9 +15,13 @@
 
 
 def each_peer(me, n, body):
-    if n <= 16:
-        for step in range(1, n):
-            body(lax.rem(me + step, n))
+    if n <= 16 and n & (n - 1) == 0:
+        for step in range(n - 1, 0, -1):
+            peer = me
+            for bit in (1, 2, 4, 8):
+                if step & bit:
+                    peer = peer + bit - 2 * bit * lax.rem(me // bit, 2)
+            body(peer)
     else:
 
         @pl.loop(1, n)
@@ -26,7 +30,7 @@
 
 
 def kernel(
-    n, values, rows_in, cols_in, live_in, bias_in, balanced, coverage,
+    n, values, rows_in, cols_in, live_in, bias_in, plain, relative, numerator,
     tiles, rows, cols, live, bias, scales0, scales1, send0, send1, recv0, recv1,
     tile_sem, small_sem, out_sem, in_sem,
 ):
@@ -68,8 +72,8 @@
             me,
             n,
             lambda peer: pltpu.make_async_remote_copy(
-                src_ref=scales.at[me],
-                dst_ref=scales.at[me],
+                src_ref=scales.at[me, pl.ds(0, parts)],
+                dst_ref=scales.at[me, pl.ds(0, parts)],
                 send_sem=out_sem.at[phase],
                 recv_sem=in_sem.at[phase],
                 device_id=(group, peer),
@@ -82,8 +86,8 @@
             me,
             n,
             lambda peer: pltpu.make_async_remote_copy(
-                src_ref=send.at[peer],
-                dst_ref=recv.at[me],
+                src_ref=send.at[peer, pl.ds(0, messages)],
+                dst_ref=recv.at[me, pl.ds(0, messages)],
                 send_sem=out_sem.at[phase],
                 recv_sem=in_sem.at[phase],
                 device_id=(group, peer),
@@ -91,8 +95,8 @@
             ).start(),
         )
 
-    def arrived(buffer, sem):
-        every = buffer.at[pl.ds(0, n - 1)]
+    def arrived(buffer, sem, count):
+        every = buffer.at[pl.ds(0, n - 1), pl.ds(0, count)]
         pltpu.make_async_copy(every, every, sem).wait()
 
     def as_row(buffer, index):
@@ -154,7 +158,7 @@
             for copy in loads[BAND:]:
                 copy.wait()
 
-        arrived(scales, in_sem.at[2 * sweep])
+        arrived(scales, in_sem.at[2 * sweep], parts)
         to_rows = jnp.zeros((n, width), jnp.float32)
         for extra in range(TRANS):
             slot = held + extra
@@ -186,7 +190,7 @@
         for part in range(parts):
             recv[me, part : part + 1, :] = owned[:, part * LANES : (part + 1) * LANES]
         recv[me, parts:messages, :] = form
-        arrived(recv, in_sem.at[2 * sweep + 1])
+        arrived(recv, in_sem.at[2 * sweep + 1], messages)
         total = jnp.sum(recv[:, 0:messages, :], axis=0)
         grands.append(2.0 * jnp.sum(total[parts:messages], keepdims=True))
         total = total[0:parts]
@@ -195,14 +199,15 @@
             scales1[me, 0:parts, :] = mine
 
     bins = float(n * width)
-    over = mine * total * (bins / grands[1])
-    result = mine * (grands[0] / bins) / over
+    factor = total * (bins / grands[1])
+    raised = mine * (grands[0] / bins)
     for part in range(parts):
         lanes = slice(part * LANES, (part + 1) * LANES)
-        coverage[:, lanes] = over[part : part + 1]
-        balanced[:, lanes] = result[part : part + 1]
+        plain[:, lanes] = mine[part : part + 1]
+        relative[:, lanes] = factor[part : part + 1]
+        numerator[:, lanes] = raised[part : part + 1]
     for phase, buffer in enumerate((scales0, send0, scales1, send1)):
-        arrived(buffer, out_sem.at[phase])
+        arrived(buffer, out_sem.at[phase], (parts, messages)[phase % 2])
 
 
 def solution(mesh):
@@ -211,11 +216,11 @@
     def shards(tile_values, tile_rows, tile_cols, tile_live, bias):
         slots, width = tile_values.shape[0], tile_values.shape[1]
         block = pltpu.VMEM((n, 8, LANES), jnp.float32)
-        return pl.pallas_call(
+        plain, relative, numerator = pl.pallas_call(
             functools.partial(kernel, n),
-            out_shape=(jax.ShapeDtypeStruct(bias.shape, jnp.float32),) * 2,
-            in_specs=[pl.BlockSpec(memory_space=pltpu.HBM)] * 5,
-            out_specs=(pl.BlockSpec(memory_space=pltpu.VMEM),) * 2,
+            out_shape=(jax.ShapeDtypeStruct(bias.shape, jnp.float32),) * 3,
+            in_specs=[pl.BlockSpec(memory_space=pl.ANY)] * 5,
+            out_specs=(pl.BlockSpec(memory_space=pltpu.VMEM),) * 3,
             scratch_shapes=[
                 pltpu.VMEM((slots, width, width), jnp.bfloat16),
                 pltpu.SMEM((slots,), jnp.int32),
@@ -229,9 +234,11 @@
                 pltpu.SemaphoreType.DMA((4,)),
             ],
             compiler_params=pltpu.CompilerParams(
-                collective_id=0, has_side_effects=True, vmem_limit_bytes=48 * 1024 * 1024
+                collective_id=0, has_side_effects=True, vmem_limit_bytes=64 * 1024 * 1024 - 65536
             ),
         )(tile_values, tile_rows, tile_cols, tile_live, bias)
+        coverage = plain * relative
+        return numerator / coverage, coverage
 
     placed = (
         P(("groups", "tile"), None, None),

time: 31.7 us -> 26.1 us (0.82)
  local copies, waits for them, and re-layouts: 6.28 us -> 0 us
  other arithmetic: 0 us -> 1.26 us
  Pallas kernels: 24.6 us -> 24 us
    unnamed x12 -> x0, local copies, waits for them, and re-layouts: 6.28 us -> none
    div x0 -> x1, other arithmetic: none -> 1.26 us  [shards(): return (numerator / coverage, coverage)]
    pallas_call x1, Pallas kernels: 24.6 us -> 24 us  [shards(): pl.pallas_call(functools.partial(kernel, n), out_shape=(jax.ShapeDtypeStr...]
where the time goes in v2:
time: 26.1 us; the launch traced here: 25.9 us
  Pallas kernels  24 us (92%)
  other arithmetic  1.26 us (5%)
  between operations  0.64 us (2%)
    pallas_call x1, Pallas kernels, shards(): pl.pallas_call(functools.partial(kernel, n), out_shape=(jax.ShapeDtypeStr...  24 us
    div x1, other arithmetic, shards(): return (numerator / coverage, coverage)  1.26 us

profile of v2, /device:TPU:0, one launch (start us, length us, event | category | flops | bytes accessed | tf_op | source)
XLA Modules:
  0.0 25.9 jit_solution(2398775881136319174)
XLA Ops:
  0.6 24.0 %shard_map.68 = (f32[1,512]{1,0:T(1,128)}, f32[1,512]{1,0:T(1,128)}, f32[1,512]{1,0:T(1,128)}) custom-call(bf16[10,512,512]{2,1,0:T(8,128)(2,1)} %values.1, s32[10]{0:T(128)} %rows_in.1, s32[10]{0:T(128)} %cols_in.1, s32[10]{0:T(128)} %live_in.1, f32[1,512]{1,0:T(1,128)} %bias_in.1), custom_call_target="tpu_custom_call" | custom-call | tf_op jit(solution)/shard_map/pallas_call | solution.py:219
  24.6 1.3 %fusion = (f32[1,512]{1,0:T(1,128)}, f32[1,512]{1,0:T(1,128)}) fusion(f32[1,512]{1,0:T(1,128)} %get-tuple-element.5, f32[1,512]{1,0:T(1,128)} %get-tuple-element.6, f32[1,512]{1,0:T(1,128)} %get-tuple-element.7), kind=kLoop, calls=%fused_computation | loop fusion | flops 1024 | bytes 10240 | tf_op jit(solution)/shard_map/div | solution.py:241

commit v3 on v2

--- a/solution.py
+++ b/solution.py
@@ -65,7 +65,6 @@
     smalls[0].wait()
     for part in range(parts):
         scales0[me, part : part + 1, :] = bias[:, part * LANES : (part + 1) * LANES]
-    pl.semaphore_wait(barrier, n - 1)
 
     def gather_start(scales, phase):
         each_peer(
@@ -137,8 +136,9 @@
     for sweep, (scales, send, recv) in enumerate(
         ((scales0, send0, recv0), (scales1, send1, recv1))
     ):
-        gather_start(scales, 2 * sweep)
-        if sweep == 0:
+        if sweep > 0:
+            gather_start(scales, 2 * sweep)
+        else:
             for copy in smalls[1:]:
                 copy.wait()
             mine = scales[me, 0:parts, :]
@@ -157,6 +157,8 @@
         if sweep == 0:
             for copy in loads[BAND:]:
                 copy.wait()
+            pl.semaphore_wait(barrier, n - 1)
+            gather_start(scales, 0)
 
         arrived(scales, in_sem.at[2 * sweep], parts)
         to_rows = jnp.zeros((n, width), jnp.float32)

time: 26.1 us -> 26.1 us (level)
  no operation moved by 1% of the time
where the time goes in v3:
time: 26.1 us; the launch traced here: 25.9 us
  Pallas kernels  24 us (92%)
  other arithmetic  1.26 us (5%)
  between operations  0.64 us (2%)
    pallas_call x1, Pallas kernels, shards(): pl.pallas_call(functools.partial(kernel, n), out_shape=(jax.ShapeDtypeStr...  24 us
    div x1, other arithmetic, shards(): return (numerator / coverage, coverage)  1.26 us

profile of v3, /device:TPU:0, one launch (start us, length us, event | category | flops | bytes accessed | tf_op | source)
XLA Modules:
  0.0 25.9 jit_solution(6231350753010186771)
XLA Ops:
  0.6 24.0 %shard_map.68 = (f32[1,512]{1,0:T(1,128)}, f32[1,512]{1,0:T(1,128)}, f32[1,512]{1,0:T(1,128)}) custom-call(bf16[10,512,512]{2,1,0:T(8,128)(2,1)} %values.1, s32[10]{0:T(128)} %rows_in.1, s32[10]{0:T(128)} %cols_in.1, s32[10]{0:T(128)} %live_in.1, f32[1,512]{1,0:T(1,128)} %bias_in.1), custom_call_target="tpu_custom_call" | custom-call | tf_op jit(solution)/shard_map/pallas_call | solution.py:221
  24.6 1.3 %fusion = (f32[1,512]{1,0:T(1,128)}, f32[1,512]{1,0:T(1,128)}) fusion(f32[1,512]{1,0:T(1,128)} %get-tuple-element.5, f32[1,512]{1,0:T(1,128)} %get-tuple-element.6, f32[1,512]{1,0:T(1,128)} %get-tuple-element.7), kind=kLoop, calls=%fused_computation | loop fusion | flops 1024 | bytes 10240 | tf_op jit(solution)/shard_map/div | solution.py:243
